TPU v7x, 32 devices: a whole 2x2x4 slice. The times are simulated.
32 devices in a mesh: groups: 2 (over x), rows: 16 (over z, y, core).
Axes of the slice: x: 2, y: 2, z: 4, core: 2. Of those that a mesh axis runs over, the one named last changes fastest.
Arguments:
- hamiltonian: bfloat16 [1536, 64, 1920], P(('groups', 'rows')), parts along dimension 0, may hold values from -0.125 to 0.125
- column_blocks: int32 [1536, 30], P(('groups', 'rows')), parts along dimension 0, may hold values from 0 to 767, as said below
- block_counts: int32 [1536], P(('groups', 'rows')), parts along dimension 0, may hold values from 1 to 30, as said below
- trial_vectors: bfloat16 [1536, 64, 128], P(('groups', 'rows')), parts along dimension 0, may hold values from -6 to 6
- spectral_bounds: float32 [4], P('groups'), parts along dimension 0, may hold values from -1.6 to 1.6, as said below
Outputs:
- filtered: bfloat16 [1536, 64, 128], P(('groups', 'rows')), parts along dimension 0
There are 2 independent parts, one for each index of `groups`. A program takes and returns all parts, laid end to end along the dimension named above; each array names one. Nothing has to cross between parts.
Inputs may be any that keep to these rules, and one draw needn't show every extreme that they name: column_blocks[r, j] = (r + o) mod 768 where the offsets o of one row are distinct and lie in -16 to 16; offsets of both ends occur. `block_counts`: some row uses all slots and some row uses one. `spectral_bounds`: lower end below -0.9, upper end above 0.9.
All inputs are finite; a program needn't handle non-finite values.
Results may differ from a plain program's by a relative error of at most 0.0041.
Values may be sent and summed in bfloat16 or wider, within the bound.
A program may use at most 256 MiB of HBM per device.

v0:
```python
import jax
import jax.numpy as jnp
from jax import lax
from jax.sharding import PartitionSpec as P

REACH = 16


def extended_2(block, sides, width):
    for axis, dim in sides:
        count = lax.axis_size(axis)
        forward = [(i, i + 1) for i in range(count - 1)]
        forward.append((count - 1, 0))
        backward = [(target, source) for source, target in forward]
        low = lax.ppermute(
            lax.slice_in_dim(block, block.shape[dim] - width, None, axis=dim), axis, forward
        )
        high = lax.ppermute(lax.slice_in_dim(block, 0, width, axis=dim), axis, backward)
        block = jnp.concatenate([low, block, high], axis=dim)
    return block


def extend_panels(panels):
    margin = panels.shape[0]
    extended = extended_2(panels, (("rows", 0),), margin)
    return (extended, margin)


def local(hamiltonian, column_blocks, block_counts, trial_vectors, spectral_bounds):
    local_rows = hamiltonian.shape[0]
    slot_total = column_blocks.shape[1]
    orbitals = trial_vectors.shape[1]
    vector_total = trial_vectors.shape[2]
    window_rows = local_rows + 2 * REACH
    total_blocks = local_rows * lax.axis_size("rows")
    first_block = lax.axis_index("rows") * local_rows
    valid_slot = jnp.arange(slot_total, dtype=jnp.int32)[None, :] < block_counts[:, None]
    window_index = (column_blocks - first_block + REACH + total_blocks) % total_blocks
    window_ids = jnp.arange(window_rows, dtype=jnp.int32)[None, None, :]
    selector = jnp.logical_and(valid_slot[:, :, None], window_index[:, :, None] == window_ids)
    selector = selector.astype(jnp.bfloat16)
    ham_slots = hamiltonian.reshape(local_rows, orbitals, slot_total, orbitals)
    band_matrix = jnp.einsum(
        "rjc,rajb->racb", selector, ham_slots, preferred_element_type=jnp.float32
    )
    band_matrix = band_matrix.astype(jnp.bfloat16).reshape(
        local_rows * orbitals, window_rows * orbitals
    )

    def apply_blocks(panels):
        extended, margin = extend_panels(panels)
        base = margin - REACH
        window = extended[base : base + window_rows].reshape(window_rows * orbitals, vector_total)
        product = jnp.dot(band_matrix, window, preferred_element_type=jnp.float32)
        return product.reshape(local_rows, orbitals, vector_total)

    centre = (spectral_bounds[0] + spectral_bounds[1]) / 2.0
    half_width = (spectral_bounds[1] - spectral_bounds[0]) / 2.0
    start_field = trial_vectors.astype(jnp.float32)
    product = apply_blocks(trial_vectors)
    once_filtered = ((product - centre * start_field) / half_width).astype(jnp.bfloat16)
    product = apply_blocks(once_filtered)
    filtered = (
        2.0 * (product - centre * once_filtered.astype(jnp.float32)) / half_width - start_field
    )
    return filtered.astype(jnp.bfloat16)


def solution(mesh):
    placed = (
        P(("groups", "rows"), None, None),
        P(("groups", "rows"), None),
        P(("groups", "rows")),
        P(("groups", "rows"), None, None),
        P("groups"),
    )
    return jax.shard_map(
        local,
        mesh=mesh,
        in_specs=placed,
        out_specs=P(("groups", "rows"), None, None),
        check_vma=False,
    )
```

profile of v0, /device:TPU:0, one launch (start us, length us, event | category | flops | bytes accessed | tf_op | source)
XLA Modules:
  0.0 212.3 jit_solution(5398996317943890191)
XLA Ops:
  0.0 1.6 copy.14
  1.6 5.5 %collective-permute-start.1 = (bf16[48,64,128]{2,0,1:T(8,128)(2,1)S(1)}, bf16[48,64,128]{2,0,1:T(8,128)(2,1)S(1)}, u32[]{:S(2)}, u32[]{:S(2)}) collective-permute-start(bf16[48,64,128]{2,0,1:T(8,128)(2,1)S(1)} %copy.14), channel_id=1, source_target_pairs={{1,0},{2,1},{3,2},{4,3},{5,4},{6,5},{7,6},{8,7},{9,8},{10,9},{11,1... | collective-permute-start | bytes 2359304 | tf_op jit(solution)/shard_map/ppermute | solution.py:18
  7.1 0.0 collective-permute-start
  7.1 0.0 copy-start.1
  7.1 0.0 copy-start.3
  7.2 37.1 %reshape.40 = bf16[48,64,30,64]{3,2,1,0:T(8,128)(2,1)} reshape(bf16[48,64,1920]{2,1,0:T(8,128)(2,1)} %param.5) | data formatting | bytes 23592960 | tf_op jit(solution)/shard_map/reshape | solution.py:42
  44.3 0.0 copy-done.1
  44.3 0.1 copy.13
  44.4 0.0 copy-done.3
  44.4 0.1 iota_compare_fusion.1
  44.4 0.0 copy-start.2
  44.4 0.0 copy-start
  44.5 29.2 %convert_bitcast_fusion = bf16[48,64,80,64]{2,3,1,0:T(8,128)(2,1)} fusion(bf16[48,64,30,64]{3,2,1,0:T(8,128)(2,1)} %reshape.40, s32[48,30]{1,0:T(8,128)S(1)} %copy.13, pred[48,30]{1,0:T(8,128)(4,1)S(1)} %iota_compare_fusion.1), kind=kOutput, calls=%fused_computation.2 | convolution fusion | flops 959677440 | bytes 43260960 | tf_op jit(solution)/shard_map/rjc,rajb->racb/dot_general | solution.py:43
  73.6 0.0 copy-done.2
  73.6 0.6 fusion.23
  76.8 0.0 collective-permute-done.1
  76.8 0.0 collective-permute-done
  76.8 0.0 copy-done
  76.8 33.1 %fusion.4 = bf16[48,64,128]{2,1,0:T(8,128)(2,1)} fusion(bf16[48,64,128]{2,1,0:T(8,128)(2,1)S(1)} %copy-done, bf16[48,64,80,64]{2,3,1,0:T(8,128)(2,1)} %convert_bitcast_fusion, bf16[48,64,128]{2,0,1:T(8,128)(2,1)S(1)} %collective-permute-done.1, bf16[48,64,128]{2,0,1:T(8,128)(2,1)S(1)} %copy.14, bf16[48,64,128]{2,0,1:T(8,128)(2,1)S(1)} %collective-permute-done, ...), kind=kOutput, calls=%fused_computation.7 | convolution fusion | flops 4032430080 | bytes 35389448 | tf_op jit(solution)/shard_map/dot_general | solution.py:54
  110.0 0.0 copy-start.4
  110.0 4.4 %collective-permute-start.3 = (bf16[48,64,128]{2,1,0:T(8,128)(2,1)}, bf16[48,64,128]{2,1,0:T(8,128)(2,1)S(1)}, u32[]{:S(2)}, u32[]{:S(2)}) collective-permute-start(bf16[48,64,128]{2,1,0:T(8,128)(2,1)} %fusion.4), channel_id=1, source_target_pairs={{1,0},{2,1},{3,2},{4,3},{5,4},{6,5},{7,6},{8,7},{9,8},{10,9},{11,1... | collective-permute-start | bytes 2359304 | tf_op jit(solution)/shard_map/ppermute | solution.py:18
  114.4 0.0 collective-permute-start.2
  114.4 74.0 %copy.22 = bf16[48,64,80,64]{3,1,2,0:T(8,128)(2,1)} copy(bf16[48,64,80,64]{2,3,1,0:T(8,128)(2,1)} %convert_bitcast_fusion) | data formatting | bytes 62914560 | tf_op jit(solution)/shard_map/convert_element_type | solution.py:46
  188.4 0.0 collective-permute-done.3
  188.4 0.0 collective-permute-done.2
  188.4 0.0 copy-done.4
  188.5 23.8 %fusion.5 = bf16[48,64,128]{2,1,0:T(8,128)(2,1)} fusion(bf16[48,64,128]{2,1,0:T(8,128)(2,1)S(1)} %copy-done, bf16[48,64,128]{2,1,0:T(8,128)(2,1)S(1)} %copy-done.4, bf16[48,64,80,64]{3,1,2,0:T(8,128)(2,1)} %copy.22, bf16[48,64,128]{2,1,0:T(8,128)(2,1)S(1)} %collective-permute-done.3, bf16[48,64,128]{2,1,0:T(8,128)(2,1)S(1)} %collective-permute-done.2, ...), kind=kOutput, calls=%fused_computation.8 | convolution fusion | flops 4030988288 | bytes 35389448 | tf_op jit(solution)/shard_map/dot_general | solution.py:54
  (1 shorter events, 0.0 us)
Async XLA Ops:
  1.6 75.2 %collective-permute-start.1 = (bf16[48,64,128]{2,0,1:T(8,128)(2,1)S(1)}, bf16[48,64,128]{2,0,1:T(8,128)(2,1)S(1)}, u32[]{:S(2)}, u32[]{:S(2)}) collective-permute-start(bf16[48,64,128]{2,0,1:T(8,128)(2,1)S(1)} %copy.14), channel_id=1, source_target_pairs={{1,0},{2,1},{3,2},{4,3},{5,4},{6,5},{7,6},{8,7},{9,8},{10,9},{11,1... | collective-permute-start | bytes 2359304 | tf_op jit(solution)/shard_map/ppermute | solution.py:18
  7.1 69.7 %collective-permute-start = (bf16[48,64,128]{2,0,1:T(8,128)(2,1)S(1)}, bf16[48,64,128]{2,0,1:T(8,128)(2,1)S(1)}, u32[]{:S(2)}, u32[]{:S(2)}) collective-permute-start(bf16[48,64,128]{2,0,1:T(8,128)(2,1)S(1)} %copy.14), channel_id=1, source_target_pairs={{0,1},{1,2},{2,3},{3,4},{4,5},{5,6},{6,7},{7,8},{8,9},{9,10},{10,1... | collective-permute-start | bytes 2359304 | tf_op jit(solution)/shard_map/ppermute | solution.py:15
  7.1 37.1 %copy-start.1 = (s32[48,30]{0,1:T(8,128)S(1)}, s32[48,30]{0,1:T(8,128)}, u32[]{:S(2)}) copy-start(s32[48,30]{0,1:T(8,128)} %param.6) | copy-start | bytes 17284
  7.1 37.2 %copy-start.3 = (s32[48]{0:T(128)S(1)}, s32[48]{0:T(128)}, u32[]{:S(2)}) copy-start(s32[48]{0:T(128)} %param.7) | copy-start | bytes 580
  44.4 29.2 %copy-start.2 = (f32[2]{0:T(128)S(1)}, f32[2]{0:T(128)}, u32[]{:S(2)}) copy-start(f32[2]{0:T(128)} %param.9) | copy-start | bytes 28
  44.4 32.4 %copy-start = (bf16[48,64,128]{2,1,0:T(8,128)(2,1)S(1)}, bf16[48,64,128]{2,1,0:T(8,128)(2,1)}, u32[]{:S(2)}) copy-start(bf16[48,64,128]{2,1,0:T(8,128)(2,1)} %param.8) | copy-start | bytes 2359300
  110.0 78.5 %copy-start.4 = (bf16[48,64,128]{2,1,0:T(8,128)(2,1)S(1)}, bf16[48,64,128]{2,1,0:T(8,128)(2,1)}, u32[]{:S(2)}) copy-start(bf16[48,64,128]{2,1,0:T(8,128)(2,1)} %fusion.4) | copy-start | bytes 2359300
  110.0 78.5 %collective-permute-start.3 = (bf16[48,64,128]{2,1,0:T(8,128)(2,1)}, bf16[48,64,128]{2,1,0:T(8,128)(2,1)S(1)}, u32[]{:S(2)}, u32[]{:S(2)}) collective-permute-start(bf16[48,64,128]{2,1,0:T(8,128)(2,1)} %fusion.4), channel_id=1, source_target_pairs={{1,0},{2,1},{3,2},{4,3},{5,4},{6,5},{7,6},{8,7},{9,8},{10,9},{11,1... | collective-permute-start | bytes 2359304 | tf_op jit(solution)/shard_map/ppermute | solution.py:18
  114.4 74.0 %collective-permute-start.2 = (bf16[48,64,128]{2,1,0:T(8,128)(2,1)}, bf16[48,64,128]{2,1,0:T(8,128)(2,1)S(1)}, u32[]{:S(2)}, u32[]{:S(2)}) collective-permute-start(bf16[48,64,128]{2,1,0:T(8,128)(2,1)} %fusion.4), channel_id=1, source_target_pairs={{0,1},{1,2},{2,3},{3,4},{4,5},{5,6},{6,7},{7,8},{8,9},{9,10},{10,1... | collective-permute-start | bytes 2359304 | tf_op jit(solution)/shard_map/ppermute | solution.py:15
where the time goes:
time: 215 us; the launch traced here: 212 us
  local copies, waits for them, and re-layouts  113 us (53%)
  matrix products  86.2 us (40%)
  starting transfers between devices  9.94 us (5%)
  between operations  2.6 us (1%)
    convert_element_type x1, local copies, waits for them, and re-layouts, local(): band_matrix.astype(jnp.bfloat16)  74 us
    dot_general x2, matrix products, apply_blocks(): product = jnp.dot(band_matrix, window, preferred_element_type=jnp.float32)  57 us
    reshape x1, local copies, waits for them, and re-layouts, local(): ham_slots = hamiltonian.reshape(local_rows, orbitals, slot_total, orbitals)  37.1 us
    dot_general x1, matrix products, local(): jnp.einsum('rjc,rajb->racb', selector, ham_slots, preferred_element_type=...  29.2 us
    ppermute x2, starting transfers between devices, extended_2(): lax.ppermute(lax.slice_in_dim(block, 0, width, axis=dim), axis, backward)  9.94 us
  transfers between devices with their start and end apart: 4, of which 0 were waited for; matrix products, arithmetic and copies ran while one was open for 66% of the time, Pallas kernels for 0%

commit v1 on v0

v1 whole, which is shorter than its diff:
```python
import jax
import jax.numpy as jnp
from jax import lax
from jax.experimental import pallas as pl
from jax.experimental.pallas import tpu as pltpu
from jax.sharding import PartitionSpec as P

REACH = 16
HALF = REACH // 2
CH = 4


def kernel(idx_ref, bounds_ref, h_hbm, tv_hbm, out_ref, hv, win1, win2,
           rl1, rh1, rl2, rh2, h_sem, tv_sem, send_sem, recv_sem):
    rows = h_hbm.shape[0]
    slots = idx_ref.shape[0]
    window = rows + 2 * REACH
    lo_end, hi_start = REACH, rows - REACH
    n = lax.axis_size("rows")
    me = lax.axis_index("rows")
    right, left = lax.rem(me + 1, n), lax.rem(me + n - 1, n)

    order = (list(range(lo_end, hi_start, CH))
             + list(range(HALF, lo_end, CH)) + list(range(hi_start, hi_start + HALF, CH))
             + list(range(0, HALF, CH)) + list(range(hi_start + HALF, rows, CH)))

    def h_copy(chunk):
        return pltpu.make_async_copy(
            h_hbm.at[pl.ds(chunk * CH, CH)], hv.at[pl.ds(chunk * CH, CH)], h_sem.at[chunk])

    tv_copy = pltpu.make_async_copy(tv_hbm, win1.at[pl.ds(REACH, rows)], tv_sem)
    tv_copy.start()
    for row in order[:2]:
        h_copy(row // CH).start()

    barrier = pltpu.get_barrier_semaphore()
    for neighbour in (left, right):
        pl.semaphore_signal(barrier, inc=1, device_id={"rows": neighbour},
                            device_id_type=pl.DeviceIdType.MESH)
    for row in order[2:]:
        h_copy(row // CH).start()
    zero = jnp.zeros(win1.shape[1:], win1.dtype)
    win1[window] = zero
    win2[window] = zero
    pl.semaphore_wait(barrier, 2)

    def remote(src, dst, k, target):
        return pltpu.make_async_remote_copy(
            src_ref=src, dst_ref=dst, send_sem=send_sem.at[k], recv_sem=recv_sem.at[k],
            device_id={"rows": target}, device_id_type=pl.DeviceIdType.MESH)

    def halo(src, base, low, high, k):
        return (
            remote(src.at[pl.ds(base + rows - HALF, HALF)], low.at[pl.ds(HALF, HALF)], k, right),
            remote(src.at[pl.ds(base, HALF)], high.at[pl.ds(0, HALF)], k + 1, left),
            remote(src.at[pl.ds(base + hi_start, HALF)], low.at[pl.ds(0, HALF)], k + 2, right),
            remote(src.at[pl.ds(base + HALF, HALF)], high.at[pl.ds(HALF, HALF)], k + 3, left),
        )

    first = halo(tv_hbm, 0, rl1, rh1, 0)
    second = halo(win2, REACH, rl2, rh2, 4)
    for copy in first:
        copy.start()

    centre = (bounds_ref[0] + bounds_ref[1]) * 0.5
    half = (bounds_ref[1] - bounds_ref[0]) * 0.5
    inv = 1.0 / jnp.full((1, win1.shape[2]), half, jnp.float32)

    def product(r, win):
        gathered = jnp.concatenate([win[idx_ref[j, r]] for j in range(slots)], axis=0)
        return jnp.dot(hv[r], gathered, preferred_element_type=jnp.float32)

    def one(r):
        v = win1[REACH + r].astype(jnp.float32)
        win2[REACH + r] = ((product(r, win1) - centre * v) * inv).astype(win2.dtype)

    def two(r):
        v = win2[REACH + r].astype(jnp.float32)
        start = win1[REACH + r].astype(jnp.float32)
        out_ref[r] = (2.0 * (product(r, win2) - centre * v) * inv - start).astype(out_ref.dtype)

    def run_one(low, high):
        def body(c, carry):
            h_copy(c).wait()
            for k in range(CH):
                one(c * CH + k)
            return carry
        lax.fori_loop(low // CH, high // CH, body, 0)

    def run_two(low, high):
        def body(c, carry):
            for k in range(CH):
                two(c * CH + k)
            return carry
        lax.fori_loop(low // CH, high // CH, body, 0)

    tv_copy.wait()
    run_one(lo_end, hi_start)
    first[0].wait_recv()
    win1[pl.ds(HALF, HALF)] = rl1[pl.ds(HALF, HALF)]
    run_one(HALF, lo_end)
    second[3].start()
    first[1].wait_recv()
    win1[pl.ds(REACH + rows, HALF)] = rh1[pl.ds(0, HALF)]
    run_one(hi_start, hi_start + HALF)
    second[2].start()
    first[2].wait_recv()
    win1[pl.ds(0, HALF)] = rl1[pl.ds(0, HALF)]
    run_one(0, HALF)
    second[1].start()
    first[3].wait_recv()
    win1[pl.ds(REACH + rows + HALF, HALF)] = rh1[pl.ds(HALF, HALF)]
    run_one(hi_start + HALF, rows)
    second[0].start()

    run_two(lo_end, hi_start)
    second[3].wait_recv()
    second[1].wait_recv()
    win2[pl.ds(REACH + rows, REACH)] = rh2[...]
    run_two(hi_start, rows)
    second[2].wait_recv()
    second[0].wait_recv()
    win2[pl.ds(0, REACH)] = rl2[...]
    run_two(0, lo_end)
    for copy in first + second:
        copy.wait_send()


def local(hamiltonian, column_blocks, block_counts, trial_vectors, spectral_bounds):
    rows, slots = column_blocks.shape
    orbitals, vectors = trial_vectors.shape[1:]
    window = rows + 2 * REACH
    total = rows * lax.axis_size("rows")
    start = lax.axis_index("rows") * rows - REACH
    index = column_blocks.T - start
    index = jnp.where(index < 0, index + total, index)
    index = jnp.where(index >= total, index - total, index)
    used = jnp.arange(slots, dtype=jnp.int32)[:, None] < block_counts[None, :]
    index = jnp.where(used, index, window)

    dtype = trial_vectors.dtype
    panel = lambda count: pltpu.VMEM((count, orbitals, vectors), dtype)
    return pl.pallas_call(
        kernel,
        out_shape=jax.ShapeDtypeStruct(trial_vectors.shape, dtype),
        in_specs=[
            pl.BlockSpec(memory_space=pltpu.SMEM),
            pl.BlockSpec(memory_space=pltpu.SMEM),
            pl.BlockSpec(memory_space=pltpu.HBM),
            pl.BlockSpec(memory_space=pltpu.HBM),
        ],
        out_specs=pl.BlockSpec(memory_space=pltpu.VMEM),
        scratch_shapes=[
            pltpu.VMEM(hamiltonian.shape, hamiltonian.dtype),
            panel(window + 1), panel(window + 1),
            panel(REACH), panel(REACH), panel(REACH), panel(REACH),
            pltpu.SemaphoreType.DMA((rows // CH,)),
            pltpu.SemaphoreType.DMA,
            pltpu.SemaphoreType.DMA((8,)),
            pltpu.SemaphoreType.DMA((8,)),
        ],
        compiler_params=pltpu.CompilerParams(
            collective_id=0, has_side_effects=True, vmem_limit_bytes=56 * 1024 * 1024),
    )(index, spectral_bounds, hamiltonian, trial_vectors)


def solution(mesh):
    placed = (
        P(("groups", "rows"), None, None),
        P(("groups", "rows"), None),
        P(("groups", "rows")),
        P(("groups", "rows"), None, None),
        P("groups"),
    )
    return jax.shard_map(
        local,
        mesh=mesh,
        in_specs=placed,
        out_specs=P(("groups", "rows"), None, None),
        check_vma=False,
    )
```

time: 215 us -> 28.3 us (0.13)
  the two profiles are of different devices: /device:TPU:0 before, /device:TPU:1 now
where the time goes in v1:
time: 28.3 us; the launch traced here: 27.9 us
  Pallas kernels  24.5 us (87%)
  local copies, waits for them, and re-layouts  2.06 us (7%)
  other arithmetic  1.33 us (5%)
    pallas_call x1, Pallas kernels, local(): pl.pallas_call(kernel, out_shape=jax.ShapeDtypeStruct(trial_vectors.shape...  24.5 us
    unnamed x1, local copies, waits for them, and re-layouts  2.06 us
    select_n x1, other arithmetic, local(): index = jnp.where(used, index, window)  1.33 us

profile of v1, /device:TPU:1, one launch (start us, length us, event | category | flops | bytes accessed | tf_op | source)
XLA Modules:
  0.0 27.9 jit_solution(11366571527167369872)
XLA Ops:
  0.0 1.3 %fusion.idx_ref = s32[30,48]{1,0:T(8,128)} fusion(s32[48,30]{0,1:T(8,128)} %param.6, s32[]{:T(128)S(6)} %sub.15, s32[48]{0:T(128)} %param.7), kind=kLoop, calls=%fused_computation.2 | loop fusion | flops 12960 | bytes 11716 | tf_op jit(solution)/shard_map/jit(_where)/select_n | solution.py:139
  1.3 24.5 %shard_map.55 = bf16[48,64,128]{2,1,0:T(8,128)(2,1)} custom-call(s32[30,48]{1,0:T(8,128)} %fusion.idx_ref, f32[2]{0:T(128)} %bounds_ref.1, bf16[48,64,1920]{2,1,0:T(8,128)(2,1)} %h_hbm.1, bf16[48,64,128]{2,1,0:T(8,128)(2,1)} %tv_hbm.1), custom_call_target="tpu_custom_call" | custom-call | tf_op jit(solution)/shard_map/pallas_call | solution.py:143
  25.9 2.1 %copy.7 = bf16[48,64,128]{2,1,0:T(8,128)(2,1)} copy(bf16[48,64,128]{2,1,0:T(8,128)(2,1)} %shard_map.55) | data formatting | bytes 1572864

commit v2 on v1

v2 whole, which is shorter than its diff:
```python
import jax
import jax.numpy as jnp
from jax import lax
from jax.experimental import pallas as pl
from jax.experimental.pallas import tpu as pltpu
from jax.sharding import PartitionSpec as P

REACH = 16
CH = REACH // 2
VMEM_LIMIT = 56 * 1024 * 1024


def kernel(columns_hbm, counts_hbm, bounds_hbm, h_hbm, tv_hbm, out_ref,
           columns, counts, table, idx_ref, bounds_ref, hv, win1, win2,
           rl1, rh1, rl2, rh2, small_sem, h_sem, send_sem, recv_sem):
    rows = h_hbm.shape[0]
    slots = columns_hbm.shape[0]
    orbitals, vectors = tv_hbm.shape[1:]
    window = rows + 2 * REACH
    hi_start = rows - REACH
    low_mid, high_mid = REACH // CH, hi_start // CH
    inner = high_mid - low_mid
    chunks = rows // CH
    n = lax.axis_size("rows")
    me = lax.axis_index("rows")
    right, left = lax.rem(me + 1, n), lax.rem(me + n - 1, n)

    barrier = pltpu.get_barrier_semaphore()
    for neighbour in (left, right):
        pl.semaphore_signal(barrier, inc=1, device_id={"rows": neighbour},
                            device_id_type=pl.DeviceIdType.MESH)

    def h_copy(c):
        return pltpu.make_async_copy(
            h_hbm.at[pl.ds(c * CH, CH)], hv.at[pl.ds(c * CH, CH)], h_sem.at[c])

    small = [
        pltpu.make_async_copy(columns_hbm, columns, small_sem.at[0]),
        pltpu.make_async_copy(counts_hbm, counts, small_sem.at[1]),
        pltpu.make_async_copy(bounds_hbm, bounds_ref, small_sem.at[2]),
        pltpu.make_async_copy(tv_hbm, win1.at[pl.ds(REACH, rows)], small_sem.at[3]),
    ]
    table_copy = pltpu.make_async_copy(table, idx_ref, small_sem.at[4])
    for copy in small:
        copy.start()
    for c in ([low_mid + k for k in range(inner)]
              + [c for k in range(low_mid) for c in (low_mid - 1 - k, high_mid + k)]):
        h_copy(c).start()

    def remote(src, dst, k, target):
        return pltpu.make_async_remote_copy(
            src_ref=src, dst_ref=dst, send_sem=send_sem.at[k], recv_sem=recv_sem.at[k],
            device_id={"rows": target}, device_id_type=pl.DeviceIdType.MESH)

    def halo(src, base, low, high, k):
        return (
            remote(src.at[pl.ds(base + rows - CH, CH)], low.at[pl.ds(CH, CH)], k, right),
            remote(src.at[pl.ds(base, CH)], high.at[pl.ds(0, CH)], k + 1, left),
            remote(src.at[pl.ds(base + hi_start, CH)], low.at[pl.ds(0, CH)], k + 2, right),
            remote(src.at[pl.ds(base + CH, CH)], high.at[pl.ds(CH, CH)], k + 3, left),
        )

    first = halo(tv_hbm, 0, rl1, rh1, 0)
    second = halo(win2, REACH, rl2, rh2, 4)
    pl.semaphore_wait(barrier, 2)
    for copy in first:
        copy.start()

    small[0].wait()
    small[1].wait()
    total = rows * n
    index = columns[...] - (me * rows - REACH)
    index = jnp.where(index < 0, index + total, index)
    index = jnp.where(index >= total, index - total, index)
    used = lax.broadcasted_iota(jnp.int32, index.shape, 0) < counts[...]
    table[...] = jnp.where(used, index, window)
    table_copy.start()

    zero = jnp.zeros(win1.shape[1:], win1.dtype)
    win1[window] = zero
    win2[window] = zero
    small[2].wait()
    centre = (bounds_ref[0] + bounds_ref[1]) * 0.5
    half = (bounds_ref[1] - bounds_ref[0]) * 0.5
    inv = 1.0 / jnp.full((1, vectors), half, jnp.float32)

    def products(r, win):
        gathered = jnp.concatenate(
            [jnp.concatenate([win[idx_ref[j, r]], win[idx_ref[j, r + 1]]], axis=1)
             for j in range(slots)], axis=0)
        both = jnp.dot(jnp.concatenate([hv[r], hv[r + 1]], axis=0), gathered,
                       preferred_element_type=jnp.float32)
        return both[:orbitals, :vectors], both[orbitals:, vectors:]

    def one(c):
        for k in range(0, CH, 2):
            r = c * CH + k
            for q, product in enumerate(products(r, win1)):
                v = win1[REACH + r + q].astype(jnp.float32)
                win2[REACH + r + q] = ((product - centre * v) * inv).astype(win2.dtype)

    def two(c):
        for k in range(0, CH, 2):
            r = c * CH + k
            for q, product in enumerate(products(r, win2)):
                v = win2[REACH + r + q].astype(jnp.float32)
                start = win1[REACH + r + q].astype(jnp.float32)
                out_ref[r + q] = (2.0 * (product - centre * v) * inv - start).astype(out_ref.dtype)

    def step_one(i, carry):
        k = i - inner
        edge = jnp.where(lax.rem(k, 2) == 0, low_mid - 1 - k // 2, high_mid + k // 2)
        c = jnp.where(i < inner, low_mid + i, edge)

        @pl.when(i == inner)
        def _():
            first[0].wait_recv()
            win1[pl.ds(CH, CH)] = rl1[pl.ds(CH, CH)]

        @pl.when(i == inner + 1)
        def _():
            first[1].wait_recv()
            win1[pl.ds(REACH + rows, CH)] = rh1[pl.ds(0, CH)]

        @pl.when(i == inner + 2)
        def _():
            first[2].wait_recv()
            win1[pl.ds(0, CH)] = rl1[pl.ds(0, CH)]

        @pl.when(i == inner + 3)
        def _():
            first[3].wait_recv()
            win1[pl.ds(REACH + rows + CH, CH)] = rh1[pl.ds(CH, CH)]

        h_copy(c).wait()
        one(c)
        for at, copy in ((0, second[3]), (1, second[2]), (2, second[1]), (3, second[0])):
            @pl.when(i == inner + at)
            def _():
                copy.start()
        return carry

    def step_two(i, carry):
        c = jnp.where(i < chunks - low_mid, low_mid + i, chunks - 1 - i)

        @pl.when(i == inner)
        def _():
            second[1].wait_recv()
            win2[pl.ds(REACH + rows, CH)] = rh2[pl.ds(0, CH)]

        @pl.when(i == inner + 1)
        def _():
            second[3].wait_recv()
            win2[pl.ds(REACH + rows + CH, CH)] = rh2[pl.ds(CH, CH)]

        @pl.when(i == inner + 2)
        def _():
            second[0].wait_recv()
            win2[pl.ds(CH, CH)] = rl2[pl.ds(CH, CH)]

        @pl.when(i == inner + 3)
        def _():
            second[2].wait_recv()
            win2[pl.ds(0, CH)] = rl2[pl.ds(0, CH)]

        two(c)
        return carry

    small[3].wait()
    table_copy.wait()
    lax.fori_loop(0, chunks, step_one, 0)
    lax.fori_loop(0, chunks, step_two, 0)
    for copy in first + second:
        copy.wait_send()


def local(hamiltonian, column_blocks, block_counts, trial_vectors, spectral_bounds):
    rows, slots = column_blocks.shape
    orbitals, vectors = trial_vectors.shape[1:]
    window = rows + 2 * REACH
    dtype = trial_vectors.dtype
    panel = lambda count: pltpu.VMEM((count, orbitals, vectors), dtype)
    return pl.pallas_call(
        kernel,
        out_shape=jax.ShapeDtypeStruct(trial_vectors.shape, dtype),
        in_specs=[pl.BlockSpec(memory_space=pl.ANY)] * 5,
        out_specs=pl.BlockSpec(memory_space=pltpu.VMEM),
        scratch_shapes=[
            pltpu.VMEM((slots, rows), jnp.int32),
            pltpu.VMEM((1, rows), jnp.int32),
            pltpu.VMEM((slots, rows), jnp.int32),
            pltpu.SMEM((slots, rows), jnp.int32),
            pltpu.SMEM(spectral_bounds.shape, spectral_bounds.dtype),
            pltpu.VMEM(hamiltonian.shape, hamiltonian.dtype),
            panel(window + 1), panel(window + 1),
            panel(REACH), panel(REACH), panel(REACH), panel(REACH),
            pltpu.SemaphoreType.DMA((5,)),
            pltpu.SemaphoreType.DMA((rows // CH,)),
            pltpu.SemaphoreType.DMA((8,)),
            pltpu.SemaphoreType.DMA((8,)),
        ],
        compiler_params=pltpu.CompilerParams(
            collective_id=0, has_side_effects=True, vmem_limit_bytes=VMEM_LIMIT),
    )(column_blocks.T, block_counts.reshape(1, rows), spectral_bounds, hamiltonian, trial_vectors)


def solution(mesh):
    placed = (
        P(("groups", "rows"), None, None),
        P(("groups", "rows"), None),
        P(("groups", "rows")),
        P(("groups", "rows"), None, None),
        P("groups"),
    )
    return jax.shard_map(
        local,
        mesh=mesh,
        in_specs=placed,
        out_specs=P(("groups", "rows"), None, None),
        check_vma=False,
    )
```

time: 28.3 us -> 24.4 us (0.86)
  Pallas kernels: 24.5 us -> 22.2 us
  other arithmetic: 1.33 us -> 0 us
    pallas_call x1, Pallas kernels: 24.5 us -> 22.2 us  [local(): pl.pallas_call(kernel, out_shape=jax.ShapeDtypeStruct(trial_vectors.shape...]
    select_n x1 -> x0, other arithmetic: 1.33 us -> none  [local(): index = jnp.where(used, index, window)]
where the time goes in v2:
time: 24.4 us; the launch traced here: 24.2 us
  Pallas kernels  22.2 us (91%)
  local copies, waits for them, and re-layouts  2.06 us (8%)
    pallas_call x1, Pallas kernels, local(): pl.pallas_call(kernel, out_shape=jax.ShapeDtypeStruct(trial_vectors.shape...  22.2 us
    unnamed x1, local copies, waits for them, and re-layouts  2.06 us

profile of v2, /device:TPU:1, one launch (start us, length us, event | category | flops | bytes accessed | tf_op | source)
XLA Modules:
  0.0 24.2 jit_solution(14252915036149236469)
XLA Ops:
  0.0 22.2 %shard_map.55 = bf16[48,64,128]{2,1,0:T(8,128)(2,1)} custom-call(s32[30,48]{1,0:T(8,128)} %bitcast.2, s32[1,48]{1,0:T(1,128)} %bitcast.3, f32[2]{0:T(128)} %bounds_hbm.1, bf16[48,64,1920]{2,1,0:T(8,128)(2,1)} %h_hbm.1, bf16[48,64,128]{2,1,0:T(8,128)(2,1)} %tv_hbm.1), custom_call_target="tpu_custom_call" | custom-call | tf_op jit(solution)/shard_map/pallas_call | solution.py:183
  22.2 2.1 %copy.7 = bf16[48,64,128]{2,1,0:T(8,128)(2,1)} copy(bf16[48,64,128]{2,1,0:T(8,128)(2,1)} %shard_map.55) | data formatting | bytes 1572864

commit v3 on v2

--- a/solution.py
+++ b/solution.py
@@ -10,9 +10,9 @@
 VMEM_LIMIT = 56 * 1024 * 1024
 
 
-def kernel(columns_hbm, counts_hbm, bounds_hbm, h_hbm, tv_hbm, out_ref,
-           columns, counts, table, idx_ref, bounds_ref, hv, win1, win2,
-           rl1, rh1, rl2, rh2, small_sem, h_sem, send_sem, recv_sem):
+def kernel(columns_hbm, counts_hbm, bounds_hbm, h_hbm, tv_hbm, out_hbm,
+           columns, counts, table, idx_ref, bounds_ref, hv, win1, win2, out_ref,
+           rl1, rh1, rl2, rh2, small_sem, h_sem, out_sem, send_sem, recv_sem):
     rows = h_hbm.shape[0]
     slots = columns_hbm.shape[0]
     orbitals, vectors = tv_hbm.shape[1:]
@@ -33,6 +33,10 @@
     def h_copy(c):
         return pltpu.make_async_copy(
             h_hbm.at[pl.ds(c * CH, CH)], hv.at[pl.ds(c * CH, CH)], h_sem.at[c])
+
+    def out_copy(c):
+        return pltpu.make_async_copy(
+            out_ref.at[pl.ds(c * CH, CH)], out_hbm.at[pl.ds(c * CH, CH)], out_sem.at[c])
 
     small = [
         pltpu.make_async_copy(columns_hbm, columns, small_sem.at[0]),
@@ -107,63 +111,49 @@
                 start = win1[REACH + r + q].astype(jnp.float32)
                 out_ref[r + q] = (2.0 * (product - centre * v) * inv - start).astype(out_ref.dtype)
 
+    odd = lax.rem(me, 2)
+
+    def edge_chunk(e):
+        far = e // 2
+        return jnp.where(lax.rem(e, 2) == 0, low_mid - 1 - far, high_mid + far)
+
+    def swap_sides(e):
+        return jnp.where(odd == 1, e + 1 - 2 * lax.rem(e, 2), e)
+
     def step_one(i, carry):
-        k = i - inner
-        edge = jnp.where(lax.rem(k, 2) == 0, low_mid - 1 - k // 2, high_mid + k // 2)
-        c = jnp.where(i < inner, low_mid + i, edge)
-
-        @pl.when(i == inner)
-        def _():
-            first[0].wait_recv()
-            win1[pl.ds(CH, CH)] = rl1[pl.ds(CH, CH)]
-
-        @pl.when(i == inner + 1)
-        def _():
-            first[1].wait_recv()
-            win1[pl.ds(REACH + rows, CH)] = rh1[pl.ds(0, CH)]
-
-        @pl.when(i == inner + 2)
-        def _():
-            first[2].wait_recv()
-            win1[pl.ds(0, CH)] = rl1[pl.ds(0, CH)]
-
-        @pl.when(i == inner + 3)
-        def _():
-            first[3].wait_recv()
-            win1[pl.ds(REACH + rows + CH, CH)] = rh1[pl.ds(CH, CH)]
+        p = jnp.maximum(i - inner, 0)
+        e = swap_sides(jnp.where(p < 2, p, 5 - p))
+        c = jnp.where(i < inner, low_mid + i, edge_chunk(e))
+        halo_parts = ((0, rl1, CH, CH), (1, rh1, 0, REACH + rows),
+                      (2, rl1, 0, 0), (3, rh1, CH, REACH + rows + CH))
+        for at, source, base, target in halo_parts:
+            @pl.when(jnp.logical_and(i >= inner, e == at))
+            def _():
+                first[at].wait_recv()
+                win1[pl.ds(target, CH)] = source[pl.ds(base, CH)]
 
         h_copy(c).wait()
         one(c)
-        for at, copy in ((0, second[3]), (1, second[2]), (2, second[1]), (3, second[0])):
-            @pl.when(i == inner + at)
+        for at in range(4):
+            @pl.when(jnp.logical_and(i >= inner, e == at))
             def _():
-                copy.start()
+                second[3 - at].start()
         return carry
 
     def step_two(i, carry):
-        c = jnp.where(i < chunks - low_mid, low_mid + i, chunks - 1 - i)
-
-        @pl.when(i == inner)
-        def _():
-            second[1].wait_recv()
-            win2[pl.ds(REACH + rows, CH)] = rh2[pl.ds(0, CH)]
-
-        @pl.when(i == inner + 1)
-        def _():
-            second[3].wait_recv()
-            win2[pl.ds(REACH + rows + CH, CH)] = rh2[pl.ds(CH, CH)]
-
-        @pl.when(i == inner + 2)
-        def _():
-            second[0].wait_recv()
-            win2[pl.ds(CH, CH)] = rl2[pl.ds(CH, CH)]
-
-        @pl.when(i == inner + 3)
-        def _():
-            second[2].wait_recv()
-            win2[pl.ds(0, CH)] = rl2[pl.ds(0, CH)]
+        p = jnp.maximum(i - inner, 0)
+        e = swap_sides(1 - p // 2 + 2 * lax.rem(p, 2))
+        c = jnp.where(i < inner, low_mid + i, edge_chunk(e))
+        halo_parts = ((0, rl2, CH, CH), (1, rh2, 0, REACH + rows),
+                      (2, rl2, 0, 0), (3, rh2, CH, REACH + rows + CH))
+        for at, source, base, target in halo_parts:
+            @pl.when(jnp.logical_and(i >= inner, e == at))
+            def _():
+                second[at].wait_recv()
+                win2[pl.ds(target, CH)] = source[pl.ds(base, CH)]
 
         two(c)
+        out_copy(c).start()
         return carry
 
     small[3].wait()
@@ -172,6 +162,8 @@
     lax.fori_loop(0, chunks, step_two, 0)
     for copy in first + second:
         copy.wait_send()
+    for c in range(chunks):
+        out_copy(c).wait()
 
 
 def local(hamiltonian, column_blocks, block_counts, trial_vectors, spectral_bounds):
@@ -184,7 +176,7 @@
         kernel,
         out_shape=jax.ShapeDtypeStruct(trial_vectors.shape, dtype),
         in_specs=[pl.BlockSpec(memory_space=pl.ANY)] * 5,
-        out_specs=pl.BlockSpec(memory_space=pltpu.VMEM),
+        out_specs=pl.BlockSpec(memory_space=pl.ANY),
         scratch_shapes=[
             pltpu.VMEM((slots, rows), jnp.int32),
             pltpu.VMEM((1, rows), jnp.int32),
@@ -192,9 +184,10 @@
             pltpu.SMEM((slots, rows), jnp.int32),
             pltpu.SMEM(spectral_bounds.shape, spectral_bounds.dtype),
             pltpu.VMEM(hamiltonian.shape, hamiltonian.dtype),
-            panel(window + 1), panel(window + 1),
+            panel(window + 1), panel(window + 1), panel(rows),
             panel(REACH), panel(REACH), panel(REACH), panel(REACH),
             pltpu.SemaphoreType.DMA((5,)),
+            pltpu.SemaphoreType.DMA((rows // CH,)),
             pltpu.SemaphoreType.DMA((rows // CH,)),
             pltpu.SemaphoreType.DMA((8,)),
             pltpu.SemaphoreType.DMA((8,)),

time: 24.4 us -> 23.5 us (0.963)
  the two profiles are of different devices: /device:TPU:1 before, /device:TPU:0 now
where the time goes in v3:
time: 23.5 us; the launch traced here: 23.4 us
  Pallas kernels  21.3 us (91%)
  local copies, waits for them, and re-layouts  2.06 us (9%)
    pallas_call x1, Pallas kernels, local(): pl.pallas_call(kernel, out_shape=jax.ShapeDtypeStruct(trial_vectors.shape...  21.3 us
    unnamed x1, local copies, waits for them, and re-layouts  2.06 us

profile of v3, /device:TPU:0, one launch (start us, length us, event | category | flops | bytes accessed | tf_op | source)
XLA Modules:
  0.0 23.4 jit_solution(12874336255017174406)
XLA Ops:
  0.0 21.3 %shard_map.55 = bf16[48,64,128]{2,1,0:T(8,128)(2,1)} custom-call(s32[30,48]{1,0:T(8,128)} %bitcast.2, s32[1,48]{1,0:T(1,128)} %bitcast.3, f32[2]{0:T(128)} %bounds_hbm.1, bf16[48,64,1920]{2,1,0:T(8,128)(2,1)} %h_hbm.1, bf16[48,64,128]{2,1,0:T(8,128)(2,1)} %tv_hbm.1), custom_call_target="tpu_custom_call" | custom-call | tf_op jit(solution)/shard_map/pallas_call | solution.py:175
  21.3 2.1 %copy.7 = bf16[48,64,128]{2,1,0:T(8,128)(2,1)} copy(bf16[48,64,128]{2,1,0:T(8,128)(2,1)} %shard_map.55) | data formatting | bytes 1572864

commit v4 on v3

--- a/solution.py
+++ b/solution.py
@@ -122,7 +122,7 @@
 
     def step_one(i, carry):
         p = jnp.maximum(i - inner, 0)
-        e = swap_sides(jnp.where(p < 2, p, 5 - p))
+        e = swap_sides(1 - p // 2 + 2 * lax.rem(p, 2))
         c = jnp.where(i < inner, low_mid + i, edge_chunk(e))
         halo_parts = ((0, rl1, CH, CH), (1, rh1, 0, REACH + rows),
                       (2, rl1, 0, 0), (3, rh1, CH, REACH + rows + CH))

time: 23.5 us -> 22.5 us (0.957)
  Pallas kernels: 21.3 us -> 20.3 us
    pallas_call x1, Pallas kernels: 21.3 us -> 20.3 us  [local(): pl.pallas_call(kernel, out_shape=jax.ShapeDtypeStruct(trial_vectors.shape...]
where the time goes in v4:
time: 22.5 us; the launch traced here: 22.3 us
  Pallas kernels  20.3 us (90%)
  local copies, waits for them, and re-layouts  2.06 us (9%)
    pallas_call x1, Pallas kernels, local(): pl.pallas_call(kernel, out_shape=jax.ShapeDtypeStruct(trial_vectors.shape...  20.3 us
    unnamed x1, local copies, waits for them, and re-layouts  2.06 us

profile of v4, /device:TPU:0, one launch (start us, length us, event | category | flops | bytes accessed | tf_op | source)
XLA Modules:
  0.0 22.3 jit_solution(3017146472039657378)
XLA Ops:
  0.0 20.3 %shard_map.55 = bf16[48,64,128]{2,1,0:T(8,128)(2,1)} custom-call(s32[30,48]{1,0:T(8,128)} %bitcast.2, s32[1,48]{1,0:T(1,128)} %bitcast.3, f32[2]{0:T(128)} %bounds_hbm.1, bf16[48,64,1920]{2,1,0:T(8,128)(2,1)} %h_hbm.1, bf16[48,64,128]{2,1,0:T(8,128)(2,1)} %tv_hbm.1), custom_call_target="tpu_custom_call" | custom-call | tf_op jit(solution)/shard_map/pallas_call | solution.py:175
  20.3 2.1 %copy.7 = bf16[48,64,128]{2,1,0:T(8,128)(2,1)} copy(bf16[48,64,128]{2,1,0:T(8,128)(2,1)} %shard_map.55) | data formatting | bytes 1572864
